TPU v7x, 256 devices: a whole 4x4x8 slice. The times are simulated.
256 devices in a mesh: row: 8 (over x, y_hi), col: 32 (over y_lo, z, core).
Axes of the slice: x: 4, y: 4 (y_hi: 2, y_lo: 2; y = y_hi * 2 + y_lo), z: 8, core: 2. Of those that a mesh axis runs over, the one named last changes fastest.
Arguments:
- inputs: bfloat16 [768, 12288], P('col', 'row'), may hold values from -6 to 6
- weight_in: bfloat16 [12288, 24576], P('row', 'col'), may hold values from -0.0546875 to 0.0546875
- weight_out: bfloat16 [24576, 12288], P('col', 'row'), may hold values from -0.0390625 to 0.0390625
- cotangent: bfloat16 [768, 12288], P('col', 'row'), may hold values from -6 to 6
Outputs:
- output: bfloat16 [768, 12288], P('col', 'row')
- input_grad: bfloat16 [768, 12288], P('col', 'row')
- weight_in_grad: bfloat16 [12288, 24576], P('row', 'col')
- weight_out_grad: bfloat16 [24576, 12288], P('col', 'row')
All inputs are finite; a program needn't handle non-finite values.
Results may differ from a plain program's by a relative error of at most 0.0049.
Values may be sent and summed in bfloat16 or wider, within the bound.
A program may use at most 128 MiB of HBM per device.

v0:
```python
import math

import jax
import jax.numpy as jnp
from jax import lax
from jax.sharding import PartitionSpec as P


def gelu_value(preact):
    coeff = math.sqrt(2.0 / math.pi)
    inner = coeff * (preact + 0.044715 * preact * preact * preact)
    return 0.5 * preact * (1.0 + jnp.tanh(inner))


def gelu_slope(preact):
    coeff = math.sqrt(2.0 / math.pi)
    inner = coeff * (preact + 0.044715 * preact * preact * preact)
    tangent = jnp.tanh(inner)
    return 0.5 * (1.0 + tangent) + 0.5 * preact * (1.0 - tangent * tangent) * coeff * (
        1.0 + 3.0 * 0.044715 * preact * preact
    )


def finish_hidden(combined, hidden_width):
    preact = combined[:, :hidden_width]
    upstream = combined[:, hidden_width:]
    hidden_act = gelu_value(preact).astype(jnp.bfloat16)
    hidden_grad = (upstream * gelu_slope(preact)).astype(jnp.bfloat16)
    return (hidden_act, hidden_grad)


def body(inputs, weight_in, weight_out, cotangent):
    gathered_inputs, gathered_cotangent = (
        lax.all_gather(inputs, "col", axis=0, tiled=True),
        lax.all_gather(cotangent, "col", axis=0, tiled=True),
    )
    total_tokens = gathered_inputs.shape[0]
    hidden_width = weight_in.shape[1]
    model_block = weight_in.shape[0]
    preact = jnp.dot(gathered_inputs, weight_in, preferred_element_type=jnp.float32)
    upstream = lax.dot_general(
        gathered_cotangent, weight_out, (((1,), (1,)), ((), ())), preferred_element_type=jnp.float32
    )
    combined = lax.psum_scatter(
        jnp.concatenate([preact, upstream], axis=1), "row", scatter_dimension=0, tiled=True
    )
    local_act, local_grad = finish_hidden(combined, hidden_width)
    hidden_act, hidden_grad = (
        lax.all_gather(local_act, "row", axis=0, tiled=True),
        lax.all_gather(local_grad, "row", axis=0, tiled=True),
    )
    reduced = lax.psum_scatter(
        jnp.concatenate(
            [
                jnp.dot(hidden_act, weight_out, preferred_element_type=jnp.float32),
                lax.dot_general(
                    hidden_grad,
                    weight_in,
                    (((1,), (1,)), ((), ())),
                    preferred_element_type=jnp.float32,
                ),
            ],
            axis=1,
        ),
        "col",
        scatter_dimension=0,
        tiled=True,
    )
    output = reduced[:, :model_block].astype(jnp.bfloat16)
    input_grad = reduced[:, model_block:].astype(jnp.bfloat16)
    grad_scale = float(total_tokens) ** (-0.5)
    in_product = lax.dot_general(
        gathered_inputs, hidden_grad, (((0,), (0,)), ((), ())), preferred_element_type=jnp.float32
    )
    out_product = lax.dot_general(
        hidden_act, gathered_cotangent, (((0,), (0,)), ((), ())), preferred_element_type=jnp.float32
    )
    weight_in_grad = (in_product * grad_scale).astype(jnp.bfloat16)
    weight_out_grad = (out_product * grad_scale).astype(jnp.bfloat16)
    return (output, input_grad, weight_in_grad, weight_out_grad)


def solution(mesh):
    in_specs = (P("col", "row"), P("row", "col"), P("col", "row"), P("col", "row"))
    out_specs = (P("col", "row"), P("col", "row"), P("row", "col"), P("col", "row"))
    return jax.shard_map(body, mesh=mesh, in_specs=in_specs, out_specs=out_specs, check_vma=False)
```

profile of v0, /device:TPU:1, one launch (start us, length us, event | category | flops | bytes accessed | tf_op | source)
XLA Modules:
  0.0 511.1 jit_solution(9012027320055754472)
XLA Ops:
  7.2 0.7 all-gather.7.cloned.1.call-update
  8.0 0.7 all-gather.5.cloned.1.call-update
  8.7 70.6 %all-gather.7.cloned.1.call-done = bf16[768,1536]{1,0:T(8,128)(2,1)} async-done(((bf16[24,1536]{1,0:T(8,128)(2,1)}), bf16[768,1536]{1,0:T(8,128)(2,1)}) %all-gather.7.cloned.1.call-update) | async-done | bytes 2359312 | tf_op jit(solution)/shard_map/all_gather | solution.py:35
  79.3 5.8 %fusion.10 = f32[768,768]{0,1:T(8,128)} fusion(bf16[768,1536]{1,0:T(8,128)(2,1)} %all-gather.7.cloned.1.call-done, bf16[768,1536]{1,0:T(8,128)(2,1)} %param.6), kind=kOutput, calls=%fused_computation.17 | convolution fusion | flops 1811939328 | bytes 7077888 | tf_op jit(solution)/shard_map/dot_general | solution.py:41
  85.1 61.1 %all-gather.5.cloned.1.call-done = bf16[768,1536]{1,0:T(8,128)(2,1)} async-done(((bf16[24,1536]{1,0:T(8,128)(2,1)}), bf16[768,1536]{1,0:T(8,128)(2,1)}) %all-gather.5.cloned.1.call-update) | async-done | bytes 2359312 | tf_op jit(solution)/shard_map/all_gather | solution.py:34
  146.2 3.9 fusion.9
  150.2 2.5 pad_maximum_fusion.1
  152.6 6.1 %copy.15 = f32[768,1536]{1,0:T(8,128)} copy(f32[768,1536]{0,1:T(8,128)} %pad_maximum_fusion.1) | data formatting | bytes 9437184
  158.7 0.0 all-gather.11.cloned.1.call-start
  158.8 91.8 %reduce-scatter.7.cloned.1.call-done = f32[96,1536]{1,0:T(8,128)} async-done(((f32[768,1536]{1,0:T(8,128)}), f32[96,1536]{1,0:T(8,128)}) %reduce-scatter.7.cloned.1.call-update) | async-done | bytes 589840 | tf_op jit(solution)/shard_map/reduce_scatter | solution.py:44
  250.6 2.0 multiply_convert_fusion.2
  252.6 0.5 all-gather.9.cloned.1.call-update
  253.2 52.7 %all-gather.11.cloned.1.call-done = bf16[768,768]{1,0:T(8,128)(2,1)} async-done(((bf16[96,768]{1,0:T(8,128)(2,1)}), bf16[768,768]{1,0:T(8,128)(2,1)}) %all-gather.11.cloned.1.call-update) | async-done | bytes 1179664 | tf_op jit(solution)/shard_map/all_gather | solution.py:50
  305.9 5.4 %fusion.12 = f32[768,1536]{1,0:T(8,128)} fusion(bf16[768,768]{1,0:T(8,128)(2,1)} %all-gather.11.cloned.1.call-done, bf16[1536,768]{1,0:T(8,128)(2,1)S(1)} %copy-done), kind=kOutput, calls=%fused_computation.19 | convolution fusion | flops 1811939328 | bytes 8257536 | tf_op jit(solution)/shard_map/dot_general | solution.py:56
  311.4 50.3 %all-gather.9.cloned.1.call-done = bf16[768,768]{1,0:T(8,128)(2,1)} async-done(((bf16[96,768]{1,0:T(8,128)(2,1)}), bf16[768,768]{1,0:T(8,128)(2,1)}) %all-gather.9.cloned.1.call-update) | async-done | bytes 1179664 | tf_op jit(solution)/shard_map/all_gather | solution.py:49
  361.6 6.4 %fusion.11 = f32[768,1536]{1,0:T(8,128)} fusion(bf16[768,768]{1,0:T(8,128)(2,1)} %all-gather.9.cloned.1.call-done, bf16[768,1536]{1,0:T(8,128)(2,1)} %param.6), kind=kOutput, calls=%fused_computation.18 | convolution fusion | flops 1811939328 | bytes 8257536 | tf_op jit(solution)/shard_map/dot_general | solution.py:55
  368.1 6.9 %pad_maximum_fusion = f32[768,3072]{1,0:T(8,128)} fusion(f32[768,1536]{1,0:T(8,128)S(1)} %copy-done.1, f32[768,1536]{1,0:T(8,128)} %fusion.11), kind=kLoop, calls=%fused_computation | loop fusion | flops 2359296 | bytes 18874368 | tf_op jit(solution)/shard_map/concatenate | solution.py:53
  375.0 1.2 copy-done.3
  376.2 5.1 fusion
  381.3 4.4 copy.14
  385.7 5.3 %multiply_convert_fusion = bf16[768,1536]{1,0:T(8,128)(2,1)} fusion(bf16[768,768]{1,0:T(8,128)(2,1)S(1)} %copy-done.4, bf16[768,1536]{1,0:T(8,128)(2,1)} %all-gather.7.cloned.1.call-done), kind=kOutput, calls=%fused_computation.2 | convolution fusion | flops 1814298624 | bytes 5898240 | tf_op jit(solution)/shard_map/dot_general | solution.py:75
  390.9 111.7 %reduce-scatter.5.cloned.1.call-done = f32[24,3072]{1,0:T(8,128)} async-done(((f32[768,3072]{1,0:T(8,128)}), f32[24,3072]{1,0:T(8,128)}) %reduce-scatter.5.cloned.1.call-update) | async-done | bytes 294928 | tf_op jit(solution)/shard_map/reduce_scatter | solution.py:52
  502.6 1.0 convert.4
  503.6 0.7 fusion.8
  (17 shorter events, 0.3 us)
Async XLA Ops:
  7.2 139.1 %copy-start = (bf16[1536,768]{1,0:T(8,128)(2,1)S(1)}, bf16[1536,768]{1,0:T(8,128)(2,1)}, u32[]{:S(2)}) copy-start(bf16[1536,768]{1,0:T(8,128)(2,1)} %param.5) | copy-start | bytes 7077892
  7.2 72.1 %all-gather.7.cloned.1.call-start = ((), (), s32[]{:S(2)}) async-start(), calls=%async_computation.3 | async-start | bytes 2433024 | tf_op jit(solution)/shard_map/all_gather | solution.py:35
  7.9 138.3 %all-gather.5.cloned.1.call-start = ((), (), s32[]{:S(2)}) async-start(), calls=%async_computation.2 | async-start | bytes 2433024 | tf_op jit(solution)/shard_map/all_gather | solution.py:34
  8.7 241.9 %reduce-scatter.7.cloned.1.call-start = ((), (), s32[]{:S(2)}) async-start(), calls=%async_computation.7 | async-start | bytes 5308416 | tf_op jit(solution)/shard_map/reduce_scatter | solution.py:44
  146.2 3.9 copy-start.2
  158.7 147.2 %all-gather.11.cloned.1.call-start = ((), (), s32[]{:S(2)}) async-start(), calls=%async_computation.5 | async-start | bytes 1327104 | tf_op jit(solution)/shard_map/all_gather | solution.py:50
  252.6 109.1 %all-gather.9.cloned.1.call-start = ((), (), s32[]{:S(2)}) async-start(), calls=%async_computation.4 | async-start | bytes 1327104 | tf_op jit(solution)/shard_map/all_gather | solution.py:49
  253.1 249.5 %reduce-scatter.5.cloned.1.call-start = ((), (), s32[]{:S(2)}) async-start(), calls=%async_computation.6 | async-start | bytes 9732096 | tf_op jit(solution)/shard_map/reduce_scatter | solution.py:52
  361.6 6.4 %copy-start.1 = (f32[768,1536]{1,0:T(8,128)S(1)}, f32[768,1536]{1,0:T(8,128)}, u32[]{:S(2)}) copy-start(f32[768,1536]{1,0:T(8,128)} %fusion.12) | copy-start | bytes 14155780
  374.9 1.3 copy-start.3
  381.3 4.4 copy-start.4
Sparse Core Ops, SparseCore 0:
  9.9 69.4 all-gather.6
  81.2 64.9 all-gather.4
  158.8 91.6 reduce-scatter.6
  253.9 51.9 all-gather.10
  309.3 52.2 all-gather.8
  375.1 127.4 reduce-scatter.4
where the time goes:
time: 515 us; the launch traced here: 511 us
  waiting for transfers between devices  440 us (85%)
  matrix products  31.9 us (6%)
  between operations  14.1 us (3%)
  local copies, waits for them, and re-layouts  12.4 us (2%)
  other arithmetic  12.3 us (2%)
    reduce_scatter x1, waiting for transfers between devices, body(): lax.psum_scatter(jnp.concatenate([jnp.dot(hidden_act, weight_out, preferr...  112 us
    reduce_scatter x1, waiting for transfers between devices, body(): lax.psum_scatter(jnp.concatenate([preact, upstream], axis=1), 'row', scat...  91.8 us
    all_gather x1, waiting for transfers between devices, body(): lax.all_gather(cotangent, 'col', axis=0, tiled=True)  70.6 us
    all_gather x1, waiting for transfers between devices, body(): lax.all_gather(inputs, 'col', axis=0, tiled=True)  61.1 us
    all_gather x1, waiting for transfers between devices, body(): lax.all_gather(local_grad, 'row', axis=0, tiled=True)  52.7 us
    all_gather x1, waiting for transfers between devices, body(): lax.all_gather(local_act, 'row', axis=0, tiled=True)  50.3 us
    unnamed x12, local copies, waits for them, and re-layouts  11.7 us
  transfers between devices with their start and end apart: 6, of which 6 were waited for; matrix products, arithmetic and copies ran while one was open for 5% of the time, Pallas kernels for 0%

commit v1 on v0

v1 whole, which is shorter than its diff:
```python
import functools
import math

import jax
import jax.numpy as jnp
from jax import lax
from jax.experimental import pallas as pl
from jax.experimental.pallas import tpu as pltpu
from jax.sharding import PartitionSpec as P

NZ = 8
NX = 4
F32 = jnp.float32
BF16 = jnp.bfloat16
COEFF = math.sqrt(2.0 / math.pi)
LAST = 8


def gelu_value(preact):
    inner = COEFF * (preact + 0.044715 * preact * preact * preact)
    return 0.5 * preact * (1.0 + jnp.tanh(inner))


def gelu_slope(preact):
    inner = COEFF * (preact + 0.044715 * preact * preact * preact)
    tangent = jnp.tanh(inner)
    return 0.5 * (1.0 + tangent) + 0.5 * preact * (1.0 - tangent * tangent) * COEFF * (
        1.0 + 3.0 * 0.044715 * preact * preact
    )


def nn(a, b):
    return lax.dot_general(a, b, (((1,), (0,)), ((), ())), preferred_element_type=F32)


def nt(a, b):
    return lax.dot_general(a, b, (((1,), (1,)), ((), ())), preferred_element_type=F32)


def tn(a, b):
    return lax.dot_general(a, b, (((0,), (0,)), ((), ())), preferred_element_type=F32)


def kernel(
    scale,
    inputs, weight_in, weight_out, cotangent,
    out, igrad, wigrad, wograd,
    xp, xs, win, wout, pf, sx1, rx1, sx2, rx2, sy, ry, sc, rc, hid, otmp, oacc, sl, rl, sd, rd, grads, fin,
    loc_sem, w_ssem, w_rsem, xp_ssem, xp_rsem, ay_ssem, ay_rsem, a_ssem, a_rsem,
    x1_ssem, x1_rsem, x2_ssem, x2_rsem, y_ssem, y_rsem, c_ssem, c_rsem, g_ssem, g_rsem,
    l_ssem, l_rsem, d_ssem, d_rsem, o_lsem, o_ssem, o_rsem, f_lsem, f_ssem, f_rsem,
):
    row, col = lax.axis_index("row"), lax.axis_index("col")
    x, yh = row // 2, lax.rem(row, 2)
    yl, z, core = col // 16, lax.rem(col // 2, NZ), lax.rem(col, 2)
    other = 1 - core
    width = inputs.shape[1]
    half = width // 2
    quarter = width // 4
    twin = (row, col + 1 - 2 * core)
    ylo = (row, (1 - yl) * 16 + z * 2 + core)
    yhi = (x * 2 + 1 - yh, col)

    def zdev(step):
        return (row, yl * 16 + lax.rem(z + step + NZ, NZ) * 2 + core)

    def xdev(step):
        return (lax.rem(x + step + NX, NX) * 2 + yh, col)

    def xat(step):
        return lax.rem(x + step + NX, NX)

    def send(src, dst, ssem, rsem, dev):
        return pltpu.make_async_remote_copy(
            src_ref=src, dst_ref=dst, send_sem=ssem, recv_sem=rsem,
            device_id=dev, device_id_type=pl.DeviceIdType.MESH,
        )

    def arrived(dst, rsem):
        pltpu.make_async_copy(dst, dst, rsem).wait()

    @pl.when(core == 0)
    def _():
        pltpu.make_async_copy(weight_in, win.at[0], loc_sem.at[0]).start()
        pltpu.make_async_copy(inputs, xp.at[0], loc_sem.at[1]).start()

    @pl.when(core == 1)
    def _():
        pltpu.make_async_copy(weight_out, wout.at[1], loc_sem.at[0]).start()
        pltpu.make_async_copy(cotangent, xp.at[1], loc_sem.at[1]).start()

    barrier = pltpu.get_barrier_semaphore()
    for dev in (twin, ylo, yhi, zdev(1), zdev(-1), xdev(1), xdev(-1)):
        pl.semaphore_signal(barrier, inc=1, device_id=dev, device_id_type=pl.DeviceIdType.MESH)
    pl.semaphore_wait(barrier, 7)

    @pl.when(core == 0)
    def _():
        send(cotangent, xp.at[0], xp_ssem, xp_rsem, twin).start()
        send(weight_out, wout.at[0], w_ssem, w_rsem, twin).start()

    @pl.when(core == 1)
    def _():
        send(inputs, xp.at[1], xp_ssem, xp_rsem, twin).start()
        send(weight_in, win.at[1], w_ssem, w_rsem, twin).start()

    @pl.when(core == 0)
    def _():
        pltpu.make_async_copy(inputs, xp.at[0], loc_sem.at[1]).wait()
        send(inputs, xp.at[1], xp_ssem, xp_rsem, twin).wait_recv()

    @pl.when(core == 1)
    def _():
        pltpu.make_async_copy(cotangent, xp.at[1], loc_sem.at[1]).wait()
        send(cotangent, xp.at[0], xp_ssem, xp_rsem, twin).wait_recv()

    xs[z, yl] = jnp.concatenate([xp[0].astype(F32), xp[1].astype(F32)], axis=0).astype(BF16)

    def a_send(chunk, lo, way, step):
        block = xs.at[chunk, lo]
        dev = (row, yl * 16 + lax.rem(z + 1 - 2 * way + NZ, NZ) * 2 + core)
        return send(block, block, a_ssem.at[way, lo, step], a_rsem.at[way, lo, step], dev)

    own = xs.at[z, yl]
    send(own, own, ay_ssem, ay_rsem, ylo).start()
    a_send(z, yl, 0, 0).start()
    a_send(z, yl, 1, 0).start()
    theirs = xs.at[z, 1 - yl]
    send(theirs, theirs, ay_ssem, ay_rsem, ylo).wait_recv()
    a_send(z, 1 - yl, 0, 0).start()
    a_send(z, 1 - yl, 1, 0).start()

    @pl.when(core == 0)
    def _():
        pltpu.make_async_copy(weight_in, win.at[0], loc_sem.at[0]).wait()
        send(weight_in, win.at[1], w_ssem, w_rsem, twin).wait_recv()

    @pl.when(core == 1)
    def _():
        pltpu.make_async_copy(weight_out, wout.at[1], loc_sem.at[0]).wait()
        send(weight_out, wout.at[0], w_ssem, w_rsem, twin).wait_recv()

    def chunk_of(t):
        step = (t + 1) // 2
        return lax.rem(z + NZ + (1 - 2 * lax.rem(t, 2)) * step, NZ)

    def x1_send(c, way):
        return send(sx1.at[c, way], rx1.at[c, way], x1_ssem.at[c, way], x1_rsem.at[c, way], xdev(2 * way - 1))

    def x2_send(c, way, b):
        return send(
            sx2.at[c, way, b], rx2.at[c, way, b], x2_ssem.at[c, way, b], x2_rsem.at[c, way, b], xdev(2 * way - 1)
        )

    def y_send(c):
        return send(sy.at[c], ry.at[c], y_ssem.at[c], y_rsem.at[c], yhi)

    def c_send(c):
        return send(sc.at[c], rc.at[c], c_ssem.at[c], c_rsem.at[c], twin)

    def g_send(c, hb, b, slot, dev):
        piece = hid.at[c, hb, b]
        return send(piece, piece, g_ssem.at[c, slot], g_rsem.at[c, slot], dev)

    def l_send(c):
        return send(sl.at[c], rl.at[c], l_ssem.at[c], l_rsem.at[c], ylo)

    def during(it, lag, fn):
        t = it - lag

        @pl.when(jnp.logical_and(t >= 0, t < NZ))
        def _():
            fn(t, chunk_of(t))

    def stage_arrive(t, c):
        step = (t + 1) // 2

        @pl.when(t > 0)
        def _():
            for lo in range(2):
                way = jnp.where(t == NZ - 1, lo, 1 - lax.rem(t, 2))
                a_send(c, lo, way, step - 1).wait_recv()

                @pl.when(step < jnp.where(way == lo, 4, 3))
                def _():
                    a_send(c, lo, way, step).start()

    def stage_first(t, c):
        lhs = xs[c].reshape(96, width)

        def put(o, part):
            for j in range(2):
                pf[c, 2 * o + j] = part[:, j * quarter : (j + 1) * quarter].reshape(2, 48, quarter)

        @pl.when(core == 0)
        def _():
            for o in range(2):
                put(o, nn(lhs, win[o]))

        @pl.when(core == 1)
        def _():
            for o in range(2):
                put(o, nt(lhs, wout[o]))

        for way in range(2):
            sx1[c, way] = pf[c, xat(2), way].astype(BF16)
            x1_send(c, way).start()
        for way in range(2):
            sx2[c, way, 1 - way] = pf[c, xat(2 * way - 1), 1 - way].astype(BF16)
            x2_send(c, way, 1 - way).start()

    def stage_x2(t, c):
        for way in range(2):
            x1_send(c, way).wait_recv()
            sx2[c, way, way] = (pf[c, xat(2 * way - 1), way] + rx1[c, way].astype(F32)).astype(BF16)
            x2_send(c, way, way).start()

    def stage_y(t, c):
        for way in range(2):
            for b in range(2):
                x2_send(c, way, b).wait_recv()
        sy[c] = (
            pf[c, x, 1 - yh] + rx2[c, 0, 1 - yh].astype(F32) + rx2[c, 1, 1 - yh].astype(F32)
        )
        y_send(c).start()

    def stage_twin(t, c):
        y_send(c).wait_recv()
        sc[c] = pf[c, x, yh] + rx2[c, 0, yh].astype(F32) + rx2[c, 1, yh].astype(F32) + ry[c]
        c_send(c).start()

    def stage_gelu(t, c):
        c_send(c).wait_recv()

        @pl.when(core == 0)
        def _():
            hid[c, x, yh] = (rc[c] * gelu_slope(sc[c])).astype(BF16)

        @pl.when(core == 1)
        def _():
            hid[c, x, yh] = gelu_value(rc[c]).astype(BF16)

        g_send(c, x, yh, 0, yhi).start()
        g_send(c, x, yh, 1 + yh, xdev(1)).start()
        g_send(c, x, yh, 3 + yh, xdev(-1)).start()

    def forward(c, b):
        slot = 1 + 2 * b + b
        hb = xat(2 * b - 1)
        g_send(c, hb, b, slot, yhi).wait_recv()
        g_send(c, hb, b, 5 + b, xdev(1 - 2 * b)).start()

    def stage_spread(t, c):
        g_send(c, x, 1 - yh, 0, yhi).wait_recv()
        g_send(c, x, 1 - yh, 2 - yh, xdev(1)).start()
        g_send(c, x, 1 - yh, 4 - yh, xdev(-1)).start()
        forward(c, yh)

    def stage_spread2(t, c):
        forward(c, 1 - yh)

    def stage_second(t, c):
        g_send(c, xat(-1), 1, 2, yhi).wait_recv()
        g_send(c, xat(1), 0, 3, yhi).wait_recv()
        for b in range(2):
            g_send(c, xat(2), b, 5 + b, yhi).wait_recv()
        lhs = [
            jnp.concatenate([hid[c, 2 * o + j].reshape(96, quarter) for j in range(2)], axis=1) for o in range(2)
        ]

        @pl.when(core == 0)
        def _():
            otmp[...] = (nt(lhs[0], win[0]) + nt(lhs[1], win[1])).reshape(2, 48, width)

        @pl.when(core == 1)
        def _():
            otmp[...] = (nn(lhs[0], wout[0]) + nn(lhs[1], wout[1])).reshape(2, 48, width)

        sl[c] = otmp[1 - yl].astype(BF16)
        l_send(c).start()
        oacc[c] = otmp[yl]

    def stage_pair(t, c):
        l_send(c).wait_recv()
        oacc[c] += rl[c].astype(F32)

    stages = (
        stage_pair, stage_spread2, stage_spread, stage_gelu, stage_twin, stage_y, stage_x2, stage_arrive,
        stage_first, stage_second,
    )
    lags = (8, 6, 5, 4, 3, 2, 1, 0, 0, 7)

    def loop(it, carry):
        for fn, lag in zip(stages, lags):
            during(it, lag, fn)
        return carry

    lax.fori_loop(0, NZ + LAST, loop, 0)

    def grad_tile(o, i):
        @pl.when(core == 0)
        def _():
            lhs = xs[:, :, :, pl.ds(pl.multiple_of(i * quarter, 128), quarter)].reshape(NZ * 96, quarter)
            rhs = jnp.concatenate([hid[:, 2 * o + j].reshape(NZ * 96, quarter) for j in range(2)], axis=1)
            grads[o, i] = (tn(lhs, rhs) * scale).astype(BF16)

        @pl.when(core == 1)
        def _():
            lhs = hid[:, 2 * o + i // 2].reshape(NZ * 96, quarter)
            rhs = xs[:, :, :, pl.ds(pl.multiple_of(lax.rem(i, 2) * half, 128), half)].reshape(NZ * 96, half)
            grads[o, i] = (tn(lhs, rhs) * scale).astype(BF16)

    def grad_place(i):
        a = wigrad.at[pl.ds(pl.multiple_of(i * quarter, 128), quarter), :]
        b = wograd.at[
            pl.ds(pl.multiple_of((i // 2) * quarter, 128), quarter),
            pl.ds(pl.multiple_of(lax.rem(i, 2) * half, 128), half),
        ]
        return a, b

    def grad_send(i):
        a, b = grad_place(i)

        @pl.when(core == 0)
        def _():
            send(grads.at[1, i], a, o_ssem.at[i], o_rsem.at[i], twin).start()

        @pl.when(core == 1)
        def _():
            send(grads.at[0, i], b, o_ssem.at[i], o_rsem.at[i], twin).start()

    def grad_keep(i):
        a, b = grad_place(i)

        @pl.when(core == 0)
        def _():
            pltpu.make_async_copy(grads.at[0, i], a, o_lsem.at[i]).start()

        @pl.when(core == 1)
        def _():
            pltpu.make_async_copy(grads.at[1, i], b, o_lsem.at[i]).start()

    def grad_step(k):
        def one(i, carry):
            if k < 2:
                grad_tile(other, i)
                grad_send(i)
            else:
                grad_tile(core, i)
                grad_keep(i)
            return carry

        first = 2 * (k % 2)
        lax.fori_loop(first, first + 2, one, 0)

    streams = ((1, 0, 4), (1, half, 3), (-1, 0, 3), (-1, half, 4))

    def d_send(s, k):
        return send(sd.at[s, k], rd.at[s, k], d_ssem.at[s, k], d_rsem.at[s, k], zdev(streams[s][0]))

    for k in range(4):
        for s in (0, 3, 1, 2):
            sign, first, hops = streams[s]
            if k >= hops:
                continue
            dest = lax.rem(z + NZ + sign * (hops - k), NZ)
            value = oacc[dest, :, first : first + half]
            if k > 0:
                d_send(s, k - 1).wait_recv()
                value = value + rd[s, k - 1].astype(F32)
            sd[s, k] = value.astype(BF16)
            d_send(s, k).start()
        grad_step(k)

    for s in range(4):
        d_send(s, streams[s][2] - 1).wait_recv()
    total = oacc[z] + jnp.concatenate(
        [
            rd[0, 3].astype(F32) + rd[2, 2].astype(F32),
            rd[1, 2].astype(F32) + rd[3, 3].astype(F32),
        ],
        axis=1,
    )
    fin[0] = total[:24].astype(BF16)
    fin[1] = total[24:].astype(BF16)

    @pl.when(core == 0)
    def _():
        send(fin.at[1], igrad, f_ssem, f_rsem, twin).start()
        pltpu.make_async_copy(fin.at[0], igrad, f_lsem).start()

    @pl.when(core == 1)
    def _():
        send(fin.at[0], out, f_ssem, f_rsem, twin).start()
        pltpu.make_async_copy(fin.at[1], out, f_lsem).start()

    send(own, own, ay_ssem, ay_rsem, ylo).wait_send()
    for way in range(2):
        for lo in range(2):
            for step in range(4 if way == lo else 3):
                a_send(z, lo, way, step).wait_send()

    def drain(c, carry):
        for way in range(2):
            x1_send(c, way).wait_send()
            for b in range(2):
                x2_send(c, way, b).wait_send()
        y_send(c).wait_send()
        c_send(c).wait_send()
        for slot in range(7):
            g_send(c, x, yh, slot, yhi).wait_send()
        l_send(c).wait_send()
        return carry

    lax.fori_loop(0, NZ, drain, 0)
    for s in range(4):
        for k in range(streams[s][2]):
            d_send(s, k).wait_send()

    for c, mine, his, parcel, wbuf, slot, result, other_result, tokens in (
        (0, wigrad, wograd, weight_out, wout, 0, igrad, out, cotangent),
        (1, wograd, wigrad, weight_in, win, 1, out, igrad, inputs),
    ):
        @pl.when(core == c)
        def _():
            send(tokens, xp.at[c], xp_ssem, xp_rsem, twin).wait_send()
            send(parcel, wbuf.at[slot], w_ssem, w_rsem, twin).wait_send()
            for i in range(4):
                a, b = grad_place(i)
                keep, take = (a, b) if c == 0 else (b, a)
                pltpu.make_async_copy(grads.at[c, i], keep, o_lsem.at[i]).wait()
                send(grads.at[1 - c, i], keep, o_ssem.at[i], o_rsem.at[i], twin).wait_send()
                send(grads.at[c, i], take, o_ssem.at[i], o_rsem.at[i], twin).wait_recv()
            pltpu.make_async_copy(fin.at[c], result, f_lsem).wait()
            send(fin.at[1 - c], result, f_ssem, f_rsem, twin).wait_send()
            send(fin.at[c], other_result, f_ssem, f_rsem, twin).wait_recv()


def body(inputs, weight_in, weight_out, cotangent):
    tokens, width = inputs.shape
    hidden = weight_in.shape[1]
    quarter = width // 4
    total_tokens = tokens * 32
    dma = pltpu.SemaphoreType.DMA
    vmem = pltpu.VMEM
    piece = (48, quarter)
    scratch = [
        vmem((2, tokens, width), BF16),
        vmem((NZ, 2, 48, width), BF16),
        vmem((2, width, hidden), BF16),
        vmem((2, hidden, width), BF16),
        vmem((NZ, 4, 2) + piece, F32),
        vmem((NZ, 2) + piece, BF16),
        vmem((NZ, 2) + piece, BF16),
        vmem((NZ, 2, 2) + piece, BF16),
        vmem((NZ, 2, 2) + piece, BF16),
        vmem((NZ,) + piece, F32),
        vmem((NZ,) + piece, F32),
        vmem((NZ,) + piece, F32),
        vmem((NZ,) + piece, F32),
        vmem((NZ, 4, 2) + piece, BF16),
        vmem((2, 48, width), F32),
        vmem((NZ, 48, width), F32),
        vmem((NZ, 48, width), BF16),
        vmem((NZ, 48, width), BF16),
        vmem((4, 4, 48, width // 2), BF16),
        vmem((4, 4, 48, width // 2), BF16),
        vmem((2, 4, quarter, width // 2), BF16),
        vmem((2, tokens, width), BF16),
        dma((2,)),
        dma, dma, dma, dma, dma, dma,
        dma((2, 2, 4)), dma((2, 2, 4)),
        dma((NZ, 2)), dma((NZ, 2)),
        dma((NZ, 2, 2)), dma((NZ, 2, 2)),
        dma((NZ,)), dma((NZ,)),
        dma((NZ,)), dma((NZ,)),
        dma((NZ, 7)), dma((NZ, 7)),
        dma((NZ,)), dma((NZ,)),
        dma((4, 4)), dma((4, 4)),
        dma((4,)), dma((4,)), dma((4,)),
        dma, dma, dma,
    ]
    shapes = (inputs.shape, cotangent.shape, weight_in.shape, weight_out.shape)
    return pl.pallas_call(
        functools.partial(kernel, float(total_tokens) ** (-0.5)),
        out_shape=tuple(jax.ShapeDtypeStruct(s, BF16) for s in shapes),
        in_specs=[pl.BlockSpec(memory_space=pl.ANY)] * 4,
        out_specs=tuple([pl.BlockSpec(memory_space=pl.ANY)] * 4),
        scratch_shapes=scratch,
        compiler_params=pltpu.CompilerParams(
            collective_id=0, has_side_effects=True, vmem_limit_bytes=58 * 1024 * 1024
        ),
        name="block",
    )(inputs, weight_in, weight_out, cotangent)


def solution(mesh):
    in_specs = (P("col", "row"), P("row", "col"), P("col", "row"), P("col", "row"))
    out_specs = (P("col", "row"), P("col", "row"), P("row", "col"), P("col", "row"))
    return jax.shard_map(body, mesh=mesh, in_specs=in_specs, out_specs=out_specs, check_vma=False)
```

time: 515 us -> 131 us (0.25)
  waiting for transfers between devices: 440 us -> 0 us
  Pallas kernels: 0 us -> 123 us
  matrix products: 31.9 us -> 0 us
  between operations: 14.1 us -> 0.64 us
  other arithmetic: 12.3 us -> 0 us
    all_gather x4 -> x0, waiting for transfers between devices: 235 us -> none  [the longest x1 70.6 us: body(): lax.all_gather(cotangent, 'col', axis=0, tiled=True)]
    reduce_scatter x2 -> x0, waiting for transfers between devices: 203 us -> none  [the longest x1 112 us: body(): lax.psum_scatter(jnp.concatenate([jnp.dot(hidden_act, weight_out, preferr...]
    pallas_call x0 -> x1, Pallas kernels: none -> 123 us  [body(): pl.pallas_call(functools.partial(kernel, float(total_tokens) ** (-0.5)),...]
    dot_general x6 -> x0, matrix products: 31.9 us -> none  [the longest x1 6.41 us: body(): jnp.dot(hidden_act, weight_out, preferred_element_type=jnp.float32)]
    concatenate x2 -> x0, other arithmetic: 9.36 us -> none  [the longest x1 6.87 us: body(): jnp.concatenate([jnp.dot(hidden_act, weight_out, preferred_element_type=j...]
    unnamed x12 -> x6, local copies, waits for them, and re-layouts: 11.7 us -> 7.82 us
  transfers between devices with their start and end apart: 6 -> 0, of which waited for: 6 -> 0; matrix products, arithmetic and copies ran while one was open for 5% -> 0% of each run, Pallas kernels for 0% -> 0%
where the time goes in v1:
time: 131 us
  Pallas kernels  123 us (94%)
  local copies, waits for them, and re-layouts  7.82 us (6%)
    pallas_call x1, Pallas kernels, body(): pl.pallas_call(functools.partial(kernel, float(total_tokens) ** (-0.5)),...  123 us
    unnamed x6, local copies, waits for them, and re-layouts  7.82 us

profile of v1, /device:TPU:1, one launch (start us, length us, event | category | flops | bytes accessed | tf_op | source)
XLA Modules:
  0.0 131.2 jit_solution(936592600473686992)
XLA Ops:
  0.6 122.8 %block.1 = (bf16[24,1536]{1,0:T(8,128)(2,1)}, bf16[24,1536]{1,0:T(8,128)(2,1)}, bf16[1536,768]{1,0:T(8,128)(2,1)}, bf16[768,1536]{1,0:T(8,128)(2,1)}) custom-call(bf16[24,1536]{1,0:T(8,128)(2,1)} %inputs.1, bf16[1536,768]{1,0:T(8,128)(2,1)} %weight_in.1, bf16[768,1536]{1,0:T(8,128)(2,1)} %weight_out.1, bf16[24,1536]{1,0:T(8,128)(2,1)} %cotangent.1), custom_call_target="tpu_custom_call" | custom-call | tf_op jit(solution)/shard_map/block/pallas_call | solution.py:484
  123.4 1.5 %copy.12 = bf16[24,1536]{1,0:T(8,128)(2,1)} copy(bf16[24,1536]{1,0:T(8,128)(2,1)} %get-tuple-element.8) | data formatting | bytes 147456
  124.9 1.5 %copy.13 = bf16[24,1536]{1,0:T(8,128)(2,1)} copy(bf16[24,1536]{1,0:T(8,128)(2,1)} %get-tuple-element.9) | data formatting | bytes 147456
  126.5 0.0 copy-start
  126.5 3.4 %copy.14 = bf16[1536,768]{1,0:T(8,128)(2,1)} copy(bf16[1536,768]{1,0:T(8,128)(2,1)} %get-tuple-element.10) | data formatting | bytes 4718592
  129.8 0.0 copy-done
  129.8 1.4 %copy.15 = bf16[768,1536]{1,0:T(8,128)(2,1)} copy(bf16[768,1536]{1,0:T(8,128)(2,1)S(1)} %copy-done) | data formatting | bytes 4718592
Async XLA Ops:
  126.5 3.4 %copy-start = (bf16[768,1536]{1,0:T(8,128)(2,1)S(1)}, bf16[768,1536]{1,0:T(8,128)(2,1)}, u32[]{:S(2)}) copy-start(bf16[768,1536]{1,0:T(8,128)(2,1)} %get-tuple-element.11) | copy-start | bytes 7077892

commit v2 on v1

--- a/solution.py
+++ b/solution.py
@@ -13,7 +13,9 @@
 F32 = jnp.float32
 BF16 = jnp.bfloat16
 COEFF = math.sqrt(2.0 / math.pi)
-LAST = 8
+LAST = 4
+GATHER_BOTH = (True, True)
+REDUCE_BOTH = (False, False)
 
 
 def gelu_value(preact):
@@ -45,10 +47,10 @@
     scale,
     inputs, weight_in, weight_out, cotangent,
     out, igrad, wigrad, wograd,
-    xp, xs, win, wout, pf, sx1, rx1, sx2, rx2, sy, ry, sc, rc, hid, otmp, oacc, sl, rl, sd, rd, grads, fin,
+    xp, xs, win, wout, pf, sx1, rx1, sx2, rx2, sy, ry, sc, rc, hid, oacc, sl, rl, sd, rd, se, re, grads, fin,
     loc_sem, w_ssem, w_rsem, xp_ssem, xp_rsem, ay_ssem, ay_rsem, a_ssem, a_rsem,
     x1_ssem, x1_rsem, x2_ssem, x2_rsem, y_ssem, y_rsem, c_ssem, c_rsem, g_ssem, g_rsem,
-    l_ssem, l_rsem, d_ssem, d_rsem, o_lsem, o_ssem, o_rsem, f_lsem, f_ssem, f_rsem,
+    l_ssem, l_rsem, d_ssem, d_rsem, e_ssem, e_rsem, o_lsem, o_ssem, o_rsem, f_lsem, f_ssem, f_rsem,
 ):
     row, col = lax.axis_index("row"), lax.axis_index("col")
     x, yh = row // 2, lax.rem(row, 2)
@@ -76,9 +78,6 @@
             device_id=dev, device_id_type=pl.DeviceIdType.MESH,
         )
 
-    def arrived(dst, rsem):
-        pltpu.make_async_copy(dst, dst, rsem).wait()
-
     @pl.when(core == 0)
     def _():
         pltpu.make_async_copy(weight_in, win.at[0], loc_sem.at[0]).start()
@@ -114,21 +113,28 @@
         pltpu.make_async_copy(cotangent, xp.at[1], loc_sem.at[1]).wait()
         send(cotangent, xp.at[0], xp_ssem, xp_rsem, twin).wait_recv()
 
-    xs[z, yl] = jnp.concatenate([xp[0].astype(F32), xp[1].astype(F32)], axis=0).astype(BF16)
-
-    def a_send(chunk, lo, way, step):
-        block = xs.at[chunk, lo]
+    block = jnp.concatenate([xp[0].astype(F32), xp[1].astype(F32)], axis=0).astype(BF16)
+    for h in range(2):
+        xs[z, yl, h] = block[:, h * half : (h + 1) * half]
+
+    def ay_send(chunk, lo, h):
+        piece = xs.at[chunk, lo, h]
+        return send(piece, piece, ay_ssem.at[chunk, h], ay_rsem.at[chunk, h], ylo)
+
+    def a_send(chunk, lo, h, way, step):
+        piece = xs.at[chunk, lo, h]
         dev = (row, yl * 16 + lax.rem(z + 1 - 2 * way + NZ, NZ) * 2 + core)
-        return send(block, block, a_ssem.at[way, lo, step], a_rsem.at[way, lo, step], dev)
-
-    own = xs.at[z, yl]
-    send(own, own, ay_ssem, ay_rsem, ylo).start()
-    a_send(z, yl, 0, 0).start()
-    a_send(z, yl, 1, 0).start()
-    theirs = xs.at[z, 1 - yl]
-    send(theirs, theirs, ay_ssem, ay_rsem, ylo).wait_recv()
-    a_send(z, 1 - yl, 0, 0).start()
-    a_send(z, 1 - yl, 1, 0).start()
+        return send(piece, piece, a_ssem.at[way, lo, h, step], a_rsem.at[way, lo, h, step], dev)
+
+    for h in range(2):
+        ay_send(z, yl, h).start()
+        for way in range(2):
+            a_send(z, yl, h, way, 0).start()
+    for h in range(2):
+        ay_send(z, 1 - yl, h).wait_recv()
+        if GATHER_BOTH[h]:
+            for way in range(2):
+                a_send(z, 1 - yl, h, way, 0).start()
 
     @pl.when(core == 0)
     def _():
@@ -162,11 +168,15 @@
         piece = hid.at[c, hb, b]
         return send(piece, piece, g_ssem.at[c, slot], g_rsem.at[c, slot], dev)
 
-    def l_send(c):
-        return send(sl.at[c], rl.at[c], l_ssem.at[c], l_rsem.at[c], ylo)
+    def l_send(c, h):
+        return send(sl.at[c, h], rl.at[c, h], l_ssem.at[c, h], l_rsem.at[c, h], ylo)
 
     def during(it, lag, fn):
-        t = it - lag
+        t = 2 * (it - lag)
+
+        @pl.when(jnp.logical_and(t > 0, t <= NZ))
+        def _():
+            fn(t - 1, chunk_of(t - 1))
 
         @pl.when(jnp.logical_and(t >= 0, t < NZ))
         def _():
@@ -175,18 +185,32 @@
     def stage_arrive(t, c):
         step = (t + 1) // 2
 
+        def take(lo, h, four):
+            way = jnp.where(t == NZ - 1, four, 1 - lax.rem(t, 2))
+            a_send(c, lo, h, way, step - 1).wait_recv()
+
+            @pl.when(step < jnp.where(way == four, 4, 3))
+            def _():
+                a_send(c, lo, h, way, step).start()
+
         @pl.when(t > 0)
         def _():
-            for lo in range(2):
-                way = jnp.where(t == NZ - 1, lo, 1 - lax.rem(t, 2))
-                a_send(c, lo, way, step - 1).wait_recv()
-
-                @pl.when(step < jnp.where(way == lo, 4, 3))
-                def _():
-                    a_send(c, lo, way, step).start()
+            for h in range(2):
+                if GATHER_BOTH[h]:
+                    take(0, h, 0)
+                    take(1, h, 1)
+                else:
+                    take(yl, h, 0)
+                    ay_send(c, yl, h).start()
 
     def stage_first(t, c):
-        lhs = xs[c].reshape(96, width)
+        @pl.when(t > 0)
+        def _():
+            for h in range(2):
+                if not GATHER_BOTH[h]:
+                    ay_send(c, 1 - yl, h).wait_recv()
+
+        lhs = jnp.concatenate([xs[c, :, h].reshape(96, half) for h in range(2)], axis=1)
 
         def put(o, part):
             for j in range(2):
@@ -270,44 +294,47 @@
 
         @pl.when(core == 0)
         def _():
-            otmp[...] = (nt(lhs[0], win[0]) + nt(lhs[1], win[1])).reshape(2, 48, width)
+            oacc[c] = (nt(lhs[0], win[0]) + nt(lhs[1], win[1])).reshape(2, 48, width)
 
         @pl.when(core == 1)
         def _():
-            otmp[...] = (nn(lhs[0], wout[0]) + nn(lhs[1], wout[1])).reshape(2, 48, width)
-
-        sl[c] = otmp[1 - yl].astype(BF16)
-        l_send(c).start()
-        oacc[c] = otmp[yl]
+            oacc[c] = (nn(lhs[0], wout[0]) + nn(lhs[1], wout[1])).reshape(2, 48, width)
+
+        for h in range(2):
+            if not REDUCE_BOTH[h]:
+                sl[c, h] = oacc[c, 1 - yl, :, h * half : (h + 1) * half].astype(BF16)
+                l_send(c, h).start()
 
     def stage_pair(t, c):
-        l_send(c).wait_recv()
-        oacc[c] += rl[c].astype(F32)
+        for h in range(2):
+            if not REDUCE_BOTH[h]:
+                l_send(c, h).wait_recv()
+                oacc[c, yl, :, h * half : (h + 1) * half] += rl[c, h].astype(F32)
 
     stages = (
-        stage_pair, stage_spread2, stage_spread, stage_gelu, stage_twin, stage_y, stage_x2, stage_arrive,
-        stage_first, stage_second,
+        (stage_first, 0), (stage_y, 1), (stage_spread, 2), (stage_second, 3),
+        (stage_x2, 0), (stage_twin, 1), (stage_spread2, 2), (stage_pair, 4), (stage_gelu, 1), (stage_arrive, -1),
     )
-    lags = (8, 6, 5, 4, 3, 2, 1, 0, 0, 7)
 
     def loop(it, carry):
-        for fn, lag in zip(stages, lags):
+        for fn, lag in stages:
             during(it, lag, fn)
         return carry
 
-    lax.fori_loop(0, NZ + LAST, loop, 0)
+    lax.fori_loop(0, NZ // 2 + 1 + LAST, loop, 0)
 
     def grad_tile(o, i):
         @pl.when(core == 0)
         def _():
-            lhs = xs[:, :, :, pl.ds(pl.multiple_of(i * quarter, 128), quarter)].reshape(NZ * 96, quarter)
+            lhs = xs[:, :, i // 2, :, pl.ds(pl.multiple_of(lax.rem(i, 2) * quarter, 128), quarter)]
+            lhs = lhs.reshape(NZ * 96, quarter)
             rhs = jnp.concatenate([hid[:, 2 * o + j].reshape(NZ * 96, quarter) for j in range(2)], axis=1)
             grads[o, i] = (tn(lhs, rhs) * scale).astype(BF16)
 
         @pl.when(core == 1)
         def _():
             lhs = hid[:, 2 * o + i // 2].reshape(NZ * 96, quarter)
-            rhs = xs[:, :, :, pl.ds(pl.multiple_of(lax.rem(i, 2) * half, 128), half)].reshape(NZ * 96, half)
+            rhs = xs[:, :, lax.rem(i, 2)].reshape(NZ * 96, half)
             grads[o, i] = (tn(lhs, rhs) * scale).astype(BF16)
 
     def grad_place(i):
@@ -353,18 +380,30 @@
         first = 2 * (k % 2)
         lax.fori_loop(first, first + 2, one, 0)
 
-    streams = ((1, 0, 4), (1, half, 3), (-1, 0, 3), (-1, half, 4))
+    streams = []
+    for h in range(2):
+        for far in ((True, False) if REDUCE_BOTH[h] else (False,)):
+            longer = 1 if (h == 0) == far else -1
+            for sign in (1, -1):
+                streams.append((sign, h, far, 4 if sign == longer else 3))
+    order = sorted(range(len(streams)), key=lambda i: (not streams[i][2], -streams[i][3]))
+
+    def target(far):
+        return 1 - yl if far else yl
 
     def d_send(s, k):
         return send(sd.at[s, k], rd.at[s, k], d_ssem.at[s, k], d_rsem.at[s, k], zdev(streams[s][0]))
 
+    def e_send(h):
+        return send(se.at[h], re.at[h], e_ssem.at[h], e_rsem.at[h], ylo)
+
     for k in range(4):
-        for s in (0, 3, 1, 2):
-            sign, first, hops = streams[s]
+        for s in order:
+            sign, h, far, hops = streams[s]
             if k >= hops:
                 continue
             dest = lax.rem(z + NZ + sign * (hops - k), NZ)
-            value = oacc[dest, :, first : first + half]
+            value = oacc[dest, target(far), :, h * half : (h + 1) * half]
             if k > 0:
                 d_send(s, k - 1).wait_recv()
                 value = value + rd[s, k - 1].astype(F32)
@@ -372,15 +411,24 @@
             d_send(s, k).start()
         grad_step(k)
 
-    for s in range(4):
-        d_send(s, streams[s][2] - 1).wait_recv()
-    total = oacc[z] + jnp.concatenate(
-        [
-            rd[0, 3].astype(F32) + rd[2, 2].astype(F32),
-            rd[1, 2].astype(F32) + rd[3, 3].astype(F32),
-        ],
-        axis=1,
-    )
+    def ring_total(h, far):
+        value = oacc[z, target(far), :, h * half : (h + 1) * half]
+        for s, (_, at, away, hops) in enumerate(streams):
+            if at == h and away == far:
+                d_send(s, hops - 1).wait_recv()
+                value = value + rd[s, hops - 1].astype(F32)
+        return value
+
+    for h in range(2):
+        if REDUCE_BOTH[h]:
+            se[h] = ring_total(h, True)
+            e_send(h).start()
+    parts = [ring_total(h, False) for h in range(2)]
+    for h in range(2):
+        if REDUCE_BOTH[h]:
+            e_send(h).wait_recv()
+            parts[h] = parts[h] + re[h]
+    total = jnp.concatenate(parts, axis=1)
     fin[0] = total[:24].astype(BF16)
     fin[1] = total[24:].astype(BF16)
 
@@ -394,11 +442,16 @@
         send(fin.at[0], out, f_ssem, f_rsem, twin).start()
         pltpu.make_async_copy(fin.at[1], out, f_lsem).start()
 
-    send(own, own, ay_ssem, ay_rsem, ylo).wait_send()
     for way in range(2):
-        for lo in range(2):
-            for step in range(4 if way == lo else 3):
-                a_send(z, lo, way, step).wait_send()
+        for h in range(2):
+            for lo, four in (((0, 0), (1, 1)) if GATHER_BOTH[h] else ((yl, 0),)):
+                for step in range(4 if way == four else 3):
+                    a_send(z, lo, h, way, step).wait_send()
+    for h in range(2):
+        if GATHER_BOTH[h]:
+            ay_send(z, yl, h).wait_send()
+        if REDUCE_BOTH[h]:
+            e_send(h).wait_send()
 
     def drain(c, carry):
         for way in range(2):
@@ -409,12 +462,16 @@
         c_send(c).wait_send()
         for slot in range(7):
             g_send(c, x, yh, slot, yhi).wait_send()
-        l_send(c).wait_send()
+        for h in range(2):
+            if not GATHER_BOTH[h]:
+                ay_send(c, yl, h).wait_send()
+            if not REDUCE_BOTH[h]:
+                l_send(c, h).wait_send()
         return carry
 
     lax.fori_loop(0, NZ, drain, 0)
-    for s in range(4):
-        for k in range(streams[s][2]):
+    for s in range(len(streams)):
+        for k in range(streams[s][3]):
             d_send(s, k).wait_send()
 
     for c, mine, his, parcel, wbuf, slot, result, other_result, tokens in (
@@ -446,7 +503,7 @@
     piece = (48, quarter)
     scratch = [
         vmem((2, tokens, width), BF16),
-        vmem((NZ, 2, 48, width), BF16),
+        vmem((NZ, 2, 2, 48, width // 2), BF16),
         vmem((2, width, hidden), BF16),
         vmem((2, hidden, width), BF16),
         vmem((NZ, 4, 2) + piece, F32),
@@ -459,24 +516,27 @@
         vmem((NZ,) + piece, F32),
         vmem((NZ,) + piece, F32),
         vmem((NZ, 4, 2) + piece, BF16),
-        vmem((2, 48, width), F32),
-        vmem((NZ, 48, width), F32),
-        vmem((NZ, 48, width), BF16),
-        vmem((NZ, 48, width), BF16),
-        vmem((4, 4, 48, width // 2), BF16),
-        vmem((4, 4, 48, width // 2), BF16),
+        vmem((NZ, 2, 48, width), F32),
+        vmem((NZ, 2, 48, width // 2), BF16),
+        vmem((NZ, 2, 48, width // 2), BF16),
+        vmem((8, 4, 48, width // 2), BF16),
+        vmem((8, 4, 48, width // 2), BF16),
+        vmem((2, 48, width // 2), F32),
+        vmem((2, 48, width // 2), F32),
         vmem((2, 4, quarter, width // 2), BF16),
         vmem((2, tokens, width), BF16),
         dma((2,)),
-        dma, dma, dma, dma, dma, dma,
-        dma((2, 2, 4)), dma((2, 2, 4)),
+        dma, dma, dma, dma,
+        dma((NZ, 2)), dma((NZ, 2)),
+        dma((2, 2, 2, 4)), dma((2, 2, 2, 4)),
         dma((NZ, 2)), dma((NZ, 2)),
         dma((NZ, 2, 2)), dma((NZ, 2, 2)),
         dma((NZ,)), dma((NZ,)),
         dma((NZ,)), dma((NZ,)),
         dma((NZ, 7)), dma((NZ, 7)),
-        dma((NZ,)), dma((NZ,)),
-        dma((4, 4)), dma((4, 4)),
+        dma((NZ, 2)), dma((NZ, 2)),
+        dma((8, 4)), dma((8, 4)),
+        dma((2,)), dma((2,)),
         dma((4,)), dma((4,)), dma((4,)),
         dma, dma, dma,
     ]

time: 131 us -> 115 us (0.88)
  Pallas kernels: 123 us -> 106 us
    pallas_call x1, Pallas kernels: 123 us -> 106 us  [body(): pl.pallas_call(functools.partial(kernel, float(total_tokens) ** (-0.5)),...]
where the time goes in v2:
time: 115 us; the launch traced here: 114 us
  Pallas kernels  106 us (92%)
  local copies, waits for them, and re-layouts  7.82 us (7%)
    pallas_call x1, Pallas kernels, body(): pl.pallas_call(functools.partial(kernel, float(total_tokens) ** (-0.5)),...  106 us
    unnamed x6, local copies, waits for them, and re-layouts  7.82 us

profile of v2, /device:TPU:1, one launch (start us, length us, event | category | flops | bytes accessed | tf_op | source)
XLA Modules:
  0.0 114.4 jit_solution(13853044041774800692)
XLA Ops:
  0.6 106.0 %block.1 = (bf16[24,1536]{1,0:T(8,128)(2,1)}, bf16[24,1536]{1,0:T(8,128)(2,1)}, bf16[1536,768]{1,0:T(8,128)(2,1)}, bf16[768,1536]{1,0:T(8,128)(2,1)}) custom-call(bf16[24,1536]{1,0:T(8,128)(2,1)} %inputs.1, bf16[1536,768]{1,0:T(8,128)(2,1)} %weight_in.1, bf16[768,1536]{1,0:T(8,128)(2,1)} %weight_out.1, bf16[24,1536]{1,0:T(8,128)(2,1)} %cotangent.1), custom_call_target="tpu_custom_call" | custom-call | tf_op jit(solution)/shard_map/block/pallas_call | solution.py:544
  106.6 1.5 %copy.12 = bf16[24,1536]{1,0:T(8,128)(2,1)} copy(bf16[24,1536]{1,0:T(8,128)(2,1)} %get-tuple-element.8) | data formatting | bytes 147456
  108.1 1.5 %copy.13 = bf16[24,1536]{1,0:T(8,128)(2,1)} copy(bf16[24,1536]{1,0:T(8,128)(2,1)} %get-tuple-element.9) | data formatting | bytes 147456
  109.6 0.0 copy-start
  109.6 3.4 %copy.14 = bf16[1536,768]{1,0:T(8,128)(2,1)} copy(bf16[1536,768]{1,0:T(8,128)(2,1)} %get-tuple-element.10) | data formatting | bytes 4718592
  113.0 0.0 copy-done
  113.0 1.4 %copy.15 = bf16[768,1536]{1,0:T(8,128)(2,1)} copy(bf16[768,1536]{1,0:T(8,128)(2,1)S(1)} %copy-done) | data formatting | bytes 4718592
Async XLA Ops:
  109.6 3.4 %copy-start = (bf16[768,1536]{1,0:T(8,128)(2,1)S(1)}, bf16[768,1536]{1,0:T(8,128)(2,1)}, u32[]{:S(2)}) copy-start(bf16[768,1536]{1,0:T(8,128)(2,1)} %get-tuple-element.11) | copy-start | bytes 7077892

commit v3 on v2

--- a/solution.py
+++ b/solution.py
@@ -13,9 +13,8 @@
 F32 = jnp.float32
 BF16 = jnp.bfloat16
 COEFF = math.sqrt(2.0 / math.pi)
-LAST = 4
-GATHER_BOTH = (True, True)
-REDUCE_BOTH = (False, False)
+LAST = 3
+REDUCE_BOTH = (True, False)
 
 
 def gelu_value(preact):
@@ -48,7 +47,7 @@
     inputs, weight_in, weight_out, cotangent,
     out, igrad, wigrad, wograd,
     xp, xs, win, wout, pf, sx1, rx1, sx2, rx2, sy, ry, sc, rc, hid, oacc, sl, rl, sd, rd, se, re, grads, fin,
-    loc_sem, w_ssem, w_rsem, xp_ssem, xp_rsem, ay_ssem, ay_rsem, a_ssem, a_rsem,
+    loc_sem, w_ssem, w_rsem, xp_ssem, xp_rsem, a_ssem, a_rsem,
     x1_ssem, x1_rsem, x2_ssem, x2_rsem, y_ssem, y_rsem, c_ssem, c_rsem, g_ssem, g_rsem,
     l_ssem, l_rsem, d_ssem, d_rsem, e_ssem, e_rsem, o_lsem, o_ssem, o_rsem, f_lsem, f_ssem, f_rsem,
 ):
@@ -62,6 +61,7 @@
     twin = (row, col + 1 - 2 * core)
     ylo = (row, (1 - yl) * 16 + z * 2 + core)
     yhi = (x * 2 + 1 - yh, col)
+    ylo_twin = (row, (1 - yl) * 16 + z * 2 + other)
 
     def zdev(step):
         return (row, yl * 16 + lax.rem(z + step + NZ, NZ) * 2 + core)
@@ -81,60 +81,67 @@
     @pl.when(core == 0)
     def _():
         pltpu.make_async_copy(weight_in, win.at[0], loc_sem.at[0]).start()
-        pltpu.make_async_copy(inputs, xp.at[0], loc_sem.at[1]).start()
+        pltpu.make_async_copy(inputs, xp.at[yl, 0], loc_sem.at[1]).start()
 
     @pl.when(core == 1)
     def _():
         pltpu.make_async_copy(weight_out, wout.at[1], loc_sem.at[0]).start()
-        pltpu.make_async_copy(cotangent, xp.at[1], loc_sem.at[1]).start()
+        pltpu.make_async_copy(cotangent, xp.at[yl, 1], loc_sem.at[1]).start()
 
     barrier = pltpu.get_barrier_semaphore()
-    for dev in (twin, ylo, yhi, zdev(1), zdev(-1), xdev(1), xdev(-1)):
+    for dev in (twin, ylo, ylo_twin, yhi, zdev(1), zdev(-1), xdev(1), xdev(-1)):
         pl.semaphore_signal(barrier, inc=1, device_id=dev, device_id_type=pl.DeviceIdType.MESH)
-    pl.semaphore_wait(barrier, 7)
+    pl.semaphore_wait(barrier, 8)
+
+    def token_sends(c, mine, his):
+        slot = xp.at[yl, c]
+        return (
+            send(his, slot, xp_ssem.at[0], xp_rsem.at[0], twin),
+            send(mine, slot, xp_ssem.at[1], xp_rsem.at[1], ylo),
+            send(his, slot, xp_ssem.at[2], xp_rsem.at[2], ylo_twin),
+        )
 
     @pl.when(core == 0)
     def _():
-        send(cotangent, xp.at[0], xp_ssem, xp_rsem, twin).start()
+        for copy in token_sends(0, inputs, cotangent):
+            copy.start()
         send(weight_out, wout.at[0], w_ssem, w_rsem, twin).start()
 
     @pl.when(core == 1)
     def _():
-        send(inputs, xp.at[1], xp_ssem, xp_rsem, twin).start()
+        for copy in token_sends(1, cotangent, inputs):
+            copy.start()
         send(weight_in, win.at[1], w_ssem, w_rsem, twin).start()
 
     @pl.when(core == 0)
     def _():
-        pltpu.make_async_copy(inputs, xp.at[0], loc_sem.at[1]).wait()
-        send(inputs, xp.at[1], xp_ssem, xp_rsem, twin).wait_recv()
+        pltpu.make_async_copy(inputs, xp.at[yl, 0], loc_sem.at[1]).wait()
 
     @pl.when(core == 1)
     def _():
-        pltpu.make_async_copy(cotangent, xp.at[1], loc_sem.at[1]).wait()
-        send(cotangent, xp.at[0], xp_ssem, xp_rsem, twin).wait_recv()
-
-    block = jnp.concatenate([xp[0].astype(F32), xp[1].astype(F32)], axis=0).astype(BF16)
-    for h in range(2):
-        xs[z, yl, h] = block[:, h * half : (h + 1) * half]
-
-    def ay_send(chunk, lo, h):
-        piece = xs.at[chunk, lo, h]
-        return send(piece, piece, ay_ssem.at[chunk, h], ay_rsem.at[chunk, h], ylo)
+        pltpu.make_async_copy(cotangent, xp.at[yl, 1], loc_sem.at[1]).wait()
+
+    def build(lo):
+        block = jnp.concatenate([xp[lo, 0].astype(F32), xp[lo, 1].astype(F32)], axis=0).astype(BF16)
+        for h in range(2):
+            xs[z, lo, h] = block[:, h * half : (h + 1) * half]
 
     def a_send(chunk, lo, h, way, step):
         piece = xs.at[chunk, lo, h]
         dev = (row, yl * 16 + lax.rem(z + 1 - 2 * way + NZ, NZ) * 2 + core)
         return send(piece, piece, a_ssem.at[way, lo, h, step], a_rsem.at[way, lo, h, step], dev)
 
+    send(inputs, xp.at[yl, other], xp_ssem.at[0], xp_rsem.at[0], twin).wait_recv()
+    build(yl)
     for h in range(2):
-        ay_send(z, yl, h).start()
         for way in range(2):
             a_send(z, yl, h, way, 0).start()
+    send(inputs, xp.at[1 - yl, core], xp_ssem.at[1], xp_rsem.at[1], ylo).wait_recv()
+    send(inputs, xp.at[1 - yl, other], xp_ssem.at[2], xp_rsem.at[2], ylo_twin).wait_recv()
+    build(1 - yl)
     for h in range(2):
-        ay_send(z, 1 - yl, h).wait_recv()
-        if GATHER_BOTH[h]:
-            for way in range(2):
-                a_send(z, 1 - yl, h, way, 0).start()
+        for way in range(2):
+            a_send(z, 1 - yl, h, way, 0).start()
 
     @pl.when(core == 0)
     def _():
@@ -196,20 +203,10 @@
         @pl.when(t > 0)
         def _():
             for h in range(2):
-                if GATHER_BOTH[h]:
-                    take(0, h, 0)
-                    take(1, h, 1)
-                else:
-                    take(yl, h, 0)
-                    ay_send(c, yl, h).start()
+                take(0, h, 0)
+                take(1, h, 1)
 
     def stage_first(t, c):
-        @pl.when(t > 0)
-        def _():
-            for h in range(2):
-                if not GATHER_BOTH[h]:
-                    ay_send(c, 1 - yl, h).wait_recv()
-
         lhs = jnp.concatenate([xs[c, :, h].reshape(96, half) for h in range(2)], axis=1)
 
         def put(o, part):
@@ -311,10 +308,7 @@
                 l_send(c, h).wait_recv()
                 oacc[c, yl, :, h * half : (h + 1) * half] += rl[c, h].astype(F32)
 
-    stages = (
-        (stage_first, 0), (stage_y, 1), (stage_spread, 2), (stage_second, 3),
-        (stage_x2, 0), (stage_twin, 1), (stage_spread2, 2), (stage_pair, 4), (stage_gelu, 1), (stage_arrive, -1),
-    )
+    stages = ((stage_first, 0), (stage_y, 1), (stage_spread, 2), (stage_second, 3), (stage_x2, 0), (stage_twin, 1), (stage_spread2, 2), (stage_pair, 4), (stage_gelu, 1), (stage_arrive, -1))
 
     def loop(it, carry):
         for fn, lag in stages:
@@ -397,11 +391,19 @@
     def e_send(h):
         return send(se.at[h], re.at[h], e_ssem.at[h], e_rsem.at[h], ylo)
 
+    def waits_for_pair(s):
+        return streams[s][3] == 4 and not REDUCE_BOTH[streams[s][1]]
+
+    order.sort(key=waits_for_pair)
+    paired = False
     for k in range(4):
         for s in order:
             sign, h, far, hops = streams[s]
             if k >= hops:
                 continue
+            if waits_for_pair(s) and not paired:
+                stage_pair(NZ - 1, chunk_of(NZ - 1))
+                paired = True
             dest = lax.rem(z + NZ + sign * (hops - k), NZ)
             value = oacc[dest, target(far), :, h * half : (h + 1) * half]
             if k > 0:
@@ -444,12 +446,10 @@
 
     for way in range(2):
         for h in range(2):
-            for lo, four in (((0, 0), (1, 1)) if GATHER_BOTH[h] else ((yl, 0),)):
+            for lo, four in ((0, 0), (1, 1)):
                 for step in range(4 if way == four else 3):
                     a_send(z, lo, h, way, step).wait_send()
     for h in range(2):
-        if GATHER_BOTH[h]:
-            ay_send(z, yl, h).wait_send()
         if REDUCE_BOTH[h]:
             e_send(h).wait_send()
 
@@ -463,8 +463,6 @@
         for slot in range(7):
             g_send(c, x, yh, slot, yhi).wait_send()
         for h in range(2):
-            if not GATHER_BOTH[h]:
-                ay_send(c, yl, h).wait_send()
             if not REDUCE_BOTH[h]:
                 l_send(c, h).wait_send()
         return carry
@@ -480,7 +478,8 @@
     ):
         @pl.when(core == c)
         def _():
-            send(tokens, xp.at[c], xp_ssem, xp_rsem, twin).wait_send()
+            for k in range(3):
+                send(tokens, xp.at[yl, c], xp_ssem.at[k], xp_rsem.at[k], twin).wait_send()
             send(parcel, wbuf.at[slot], w_ssem, w_rsem, twin).wait_send()
             for i in range(4):
                 a, b = grad_place(i)
@@ -502,7 +501,7 @@
     vmem = pltpu.VMEM
     piece = (48, quarter)
     scratch = [
-        vmem((2, tokens, width), BF16),
+        vmem((2, 2, tokens, width), BF16),
         vmem((NZ, 2, 2, 48, width // 2), BF16),
         vmem((2, width, hidden), BF16),
         vmem((2, hidden, width), BF16),
@@ -526,8 +525,7 @@
         vmem((2, 4, quarter, width // 2), BF16),
         vmem((2, tokens, width), BF16),
         dma((2,)),
-        dma, dma, dma, dma,
-        dma((NZ, 2)), dma((NZ, 2)),
+        dma, dma, dma((3,)), dma((3,)),
         dma((2, 2, 2, 4)), dma((2, 2, 2, 4)),
         dma((NZ, 2)), dma((NZ, 2)),
         dma((NZ, 2, 2)), dma((NZ, 2, 2)),

time: 115 us -> 112 us (0.974)
  Pallas kernels: 106 us -> 103 us
    pallas_call x1, Pallas kernels: 106 us -> 103 us  [body(): pl.pallas_call(functools.partial(kernel, float(total_tokens) ** (-0.5)),...]
where the time goes in v3:
time: 112 us
  Pallas kernels  103 us (92%)
  local copies, waits for them, and re-layouts  7.82 us (7%)
    pallas_call x1, Pallas kernels, body(): pl.pallas_call(functools.partial(kernel, float(total_tokens) ** (-0.5)),...  103 us
    unnamed x6, local copies, waits for them, and re-layouts  7.82 us

profile of v3, /device:TPU:1, one launch (start us, length us, event | category | flops | bytes accessed | tf_op | source)
XLA Modules:
  0.0 111.9 jit_solution(6329427583968223522)
XLA Ops:
  0.6 103.4 %block.1 = (bf16[24,1536]{1,0:T(8,128)(2,1)}, bf16[24,1536]{1,0:T(8,128)(2,1)}, bf16[1536,768]{1,0:T(8,128)(2,1)}, bf16[768,1536]{1,0:T(8,128)(2,1)}) custom-call(bf16[24,1536]{1,0:T(8,128)(2,1)} %inputs.1, bf16[1536,768]{1,0:T(8,128)(2,1)} %weight_in.1, bf16[768,1536]{1,0:T(8,128)(2,1)} %weight_out.1, bf16[24,1536]{1,0:T(8,128)(2,1)} %cotangent.1), custom_call_target="tpu_custom_call" | custom-call | tf_op jit(solution)/shard_map/block/pallas_call | solution.py:542
  104.1 1.5 %copy.12 = bf16[24,1536]{1,0:T(8,128)(2,1)} copy(bf16[24,1536]{1,0:T(8,128)(2,1)} %get-tuple-element.8) | data formatting | bytes 147456
  105.6 1.5 %copy.13 = bf16[24,1536]{1,0:T(8,128)(2,1)} copy(bf16[24,1536]{1,0:T(8,128)(2,1)} %get-tuple-element.9) | data formatting | bytes 147456
  107.1 0.0 copy-start
  107.1 3.4 %copy.14 = bf16[1536,768]{1,0:T(8,128)(2,1)} copy(bf16[1536,768]{1,0:T(8,128)(2,1)} %get-tuple-element.10) | data formatting | bytes 4718592
  110.5 0.0 copy-done
  110.5 1.4 %copy.15 = bf16[768,1536]{1,0:T(8,128)(2,1)} copy(bf16[768,1536]{1,0:T(8,128)(2,1)S(1)} %copy-done) | data formatting | bytes 4718592
Async XLA Ops:
  107.1 3.4 %copy-start = (bf16[768,1536]{1,0:T(8,128)(2,1)S(1)}, bf16[768,1536]{1,0:T(8,128)(2,1)}, u32[]{:S(2)}) copy-start(bf16[768,1536]{1,0:T(8,128)(2,1)} %get-tuple-element.11) | copy-start | bytes 7077892

commit v4 on v3

--- a/solution.py
+++ b/solution.py
@@ -96,9 +96,9 @@
     def token_sends(c, mine, his):
         slot = xp.at[yl, c]
         return (
-            send(his, slot, xp_ssem.at[0], xp_rsem.at[0], twin),
             send(mine, slot, xp_ssem.at[1], xp_rsem.at[1], ylo),
             send(his, slot, xp_ssem.at[2], xp_rsem.at[2], ylo_twin),
+            send(his, slot, xp_ssem.at[0], xp_rsem.at[0], twin),
         )
 
     @pl.when(core == 0)

time: 112 us -> 112 us (level)
  no operation moved by 1% of the time
where the time goes in v4:
time: 112 us
  Pallas kernels  103 us (92%)
  local copies, waits for them, and re-layouts  7.82 us (7%)
    pallas_call x1, Pallas kernels, body(): pl.pallas_call(functools.partial(kernel, float(total_tokens) ** (-0.5)),...  103 us
    unnamed x6, local copies, waits for them, and re-layouts  7.82 us

profile of v4, /device:TPU:1, one launch (start us, length us, event | category | flops | bytes accessed | tf_op | source)
XLA Modules:
  0.0 111.8 jit_solution(4622299649166432620)
XLA Ops:
  0.6 103.3 %block.1 = (bf16[24,1536]{1,0:T(8,128)(2,1)}, bf16[24,1536]{1,0:T(8,128)(2,1)}, bf16[1536,768]{1,0:T(8,128)(2,1)}, bf16[768,1536]{1,0:T(8,128)(2,1)}) custom-call(bf16[24,1536]{1,0:T(8,128)(2,1)} %inputs.1, bf16[1536,768]{1,0:T(8,128)(2,1)} %weight_in.1, bf16[768,1536]{1,0:T(8,128)(2,1)} %weight_out.1, bf16[24,1536]{1,0:T(8,128)(2,1)} %cotangent.1), custom_call_target="tpu_custom_call" | custom-call | tf_op jit(solution)/shard_map/block/pallas_call | solution.py:542
  103.9 1.5 %copy.12 = bf16[24,1536]{1,0:T(8,128)(2,1)} copy(bf16[24,1536]{1,0:T(8,128)(2,1)} %get-tuple-element.8) | data formatting | bytes 147456
  105.4 1.5 %copy.13 = bf16[24,1536]{1,0:T(8,128)(2,1)} copy(bf16[24,1536]{1,0:T(8,128)(2,1)} %get-tuple-element.9) | data formatting | bytes 147456
  107.0 0.0 copy-start
  107.0 3.4 %copy.14 = bf16[1536,768]{1,0:T(8,128)(2,1)} copy(bf16[1536,768]{1,0:T(8,128)(2,1)} %get-tuple-element.10) | data formatting | bytes 4718592
  110.3 0.0 copy-done
  110.3 1.4 %copy.15 = bf16[768,1536]{1,0:T(8,128)(2,1)} copy(bf16[768,1536]{1,0:T(8,128)(2,1)S(1)} %copy-done) | data formatting | bytes 4718592
Async XLA Ops:
  107.0 3.4 %copy-start = (bf16[768,1536]{1,0:T(8,128)(2,1)S(1)}, bf16[768,1536]{1,0:T(8,128)(2,1)}, u32[]{:S(2)}) copy-start(bf16[768,1536]{1,0:T(8,128)(2,1)} %get-tuple-element.11) | copy-start | bytes 7077892
